TPU v7x, 32 devices: a whole 2x2x4 slice. The times are simulated.
32 devices in a mesh: grid: 8 (over y, x, core), dom: 4 (over z).
Axes of the slice: x: 2, y: 2, z: 4, core: 2. Of those that a mesh axis runs over, the one named last changes fastest.
Arguments:
- values: float32 [8, 16, 4, 4, 8, 8, 128], P('grid', 'dom'), may hold values from -2 to 2
- levels: int32 [8, 6], P('grid'), may hold values from 0 to 7, as said below
- coefficients: int32 [8], P('grid'), may hold values from -3 to 3, as said below
Outputs:
- combined: float32 [8, 16, 4, 4, 8, 8, 128], P('grid', 'dom')
Inputs may be any that keep to these rules, and one draw needn't show every extreme that they name: levels[g, k] is grid g's level along dimension k + 1. With L_k the base-two logarithm of that dimension's extent (16, 4, 4, 8, 8, 128), each entry lies between L_k - 2 and L_k, and the shortfalls L_k - levels[g, k] of one grid add up to 2 at most. `coefficients`: every coefficient is nonzero.
All inputs are finite; a program needn't handle non-finite values.
Results may differ from a plain program's by a relative error of at most 0.0003.
Values sent between devices are 32-bit elements; how exact they have to be, the bound alone decides.
A program may use at most 64 MiB of HBM per device.

v0:
```python
import jax
import jax.numpy as jnp
import numpy as np
from jax import lax
from jax.sharding import PartitionSpec as P

PRECISE = lax.Precision.HIGHEST


def coarse_position(numerator, level_now):
    while numerator > 0 and numerator % 2 == 0:
        numerator = numerator // 2
        level_now = level_now - 1
    if numerator == 0:
        return 0
    return (1 << level_now - 1) + (numerator - 1) // 2


def parent_positions(position):
    level_now = position.bit_length()
    span_size = 1 << level_now - 1
    offset = position - span_size
    return [
        coarse_position(offset % span_size, level_now - 1),
        coarse_position((offset + 1) % span_size, level_now - 1),
    ]


def hier_table(points):
    matrix = np.eye(points)
    for position in range(1, points):
        for parent in parent_positions(position):
            matrix[position, parent] -= 0.5
    return matrix


def dehier_table(points):
    matrix = np.zeros((points, points))
    matrix[0, 0] = 1.0
    for position in range(1, points):
        row_now = np.zeros(points)
        row_now[position] = 1.0
        for parent in parent_positions(position):
            row_now = row_now + 0.5 * matrix[parent]
        matrix[position] = row_now
    return matrix


def nodal_order(points):
    placed = np.zeros(points, dtype=np.int64)
    for position in range(1, points):
        level_now = position.bit_length()
        offset = position - (1 << level_now - 1)
        placed[position] = (2 * offset + 1) * points // (1 << level_now)
    return placed


def nodal_table(matrix):
    placed = nodal_order(matrix.shape[0])
    result = np.zeros(matrix.shape)
    result[placed[:, None], placed[None, :]] = matrix
    return result


def local_hier(points):
    matrix = np.zeros((points, points + 1))
    matrix[0, 0] = 1.0
    for point in range(1, points):
        stride = point & -point
        matrix[point, point] = 1.0
        matrix[point, point - stride] -= 0.5
        matrix[point, point + stride] -= 0.5
    return matrix


def local_dehier(points):
    matrix = np.zeros((points + 1, points + 1))
    matrix[0, 0] = 1.0
    matrix[points, points] = 1.0
    stride = points // 2
    while stride >= 1:
        for point in range(stride, points, 2 * stride):
            row_now = np.zeros(points + 1)
            row_now[point] = 1.0
            matrix[point] = row_now + 0.5 * (matrix[point - stride] + matrix[point + stride])
        stride = stride // 2
    return matrix[:points]


def apply_table(grid_data, matrix, dim_index):
    letters = "abcdefg"[: grid_data.ndim]
    outputs = letters[:dim_index] + "z" + letters[dim_index + 1 :]
    formula = letters + ",z" + letters[dim_index] + "->" + outputs
    return jnp.einsum(formula, grid_data, jnp.asarray(matrix, dtype=jnp.float32), precision=PRECISE)


def tail_column(column, rank_count):
    return jnp.asarray(column, dtype=jnp.float32).reshape((-1,) + (1,) * (rank_count - 1))


def holding_mask(level_row, extents):
    holding = jnp.ones(extents, dtype=jnp.float32)
    for dim_index, points in enumerate(extents):
        limit = jnp.left_shift(jnp.int32(1), level_row[dim_index])
        inside = (jnp.arange(points, dtype=jnp.int32) < limit).astype(jnp.float32)
        shape_now = [1] * len(extents)
        shape_now[dim_index] = points
        holding = holding * inside.reshape(shape_now)
    return holding


def split_rows_mask(level_count, local_rows, rank_count):
    members = lax.axis_size("dom")
    total_rows = local_rows * members
    rows_here = lax.axis_index("dom") * local_rows + jnp.arange(local_rows, dtype=jnp.int32)
    spacing = jnp.right_shift(jnp.int32(total_rows), level_count)
    inside = (jnp.remainder(rows_here, spacing) == 0).astype(jnp.float32)
    return inside.reshape((local_rows,) + (1,) * (rank_count - 1))


def split_hierarchize(grid_data):
    members = lax.axis_size("dom")
    own_index = lax.axis_index("dom")
    first_row = grid_data[0]
    all_firsts = lax.all_gather(first_row[None], "dom", axis=0, tiled=True)
    coarse = apply_table(all_firsts, nodal_table(hier_table(members)), 0)
    new_first = lax.dynamic_index_in_dim(coarse, own_index, 0, keepdims=False)
    following = lax.dynamic_index_in_dim(all_firsts, (own_index + 1) % members, 0, keepdims=False)
    local_rows = grid_data.shape[0]
    matrix = local_hier(local_rows)
    result = (
        apply_table(grid_data, matrix[:, :local_rows], 0)
        + tail_column(matrix[:, local_rows], grid_data.ndim) * following[None]
    )
    return result.at[0].set(new_first)


def split_dehierarchize(grid_data):
    members = lax.axis_size("dom")
    own_index = lax.axis_index("dom")
    first_row = grid_data[0]
    all_firsts = lax.all_gather(first_row[None], "dom", axis=0, tiled=True)
    coarse = apply_table(all_firsts, nodal_table(dehier_table(members)), 0)
    new_first = lax.dynamic_index_in_dim(coarse, own_index, 0, keepdims=False)
    following = lax.dynamic_index_in_dim(coarse, (own_index + 1) % members, 0, keepdims=False)
    local_rows = grid_data.shape[0]
    grid_data = grid_data.at[0].set(new_first)
    matrix = local_dehier(local_rows)
    return (
        apply_table(grid_data, matrix[:, :local_rows], 0)
        + tail_column(matrix[:, local_rows], grid_data.ndim) * following[None]
    )


def body(values, levels, coefficients):
    grid_data = values[0]
    level_row = levels[0]
    weight = coefficients[0].astype(jnp.float32)
    extents = tuple(grid_data.shape[1:])
    local_rows = grid_data.shape[0]
    for dim_index in range(1, 6):
        grid_data = apply_table(grid_data, hier_table(grid_data.shape[dim_index]), dim_index)
    grid_data = split_hierarchize(grid_data)
    holding = (
        split_rows_mask(level_row[0], local_rows, grid_data.ndim)
        * holding_mask(level_row[1:], extents)[None]
    )
    weighted = weight * holding * grid_data
    merged = weighted.reshape((local_rows, extents[0] * extents[1]) + extents[2:])
    own_share = lax.psum_scatter(merged, "grid", scatter_dimension=1, tiled=True)
    for dim_index in range(2, 5):
        own_share = apply_table(own_share, dehier_table(own_share.shape[dim_index]), dim_index)
    own_share = split_dehierarchize(own_share)
    gathered = lax.all_gather(own_share, "grid", axis=1, tiled=True)
    combined = gathered.reshape(grid_data.shape)
    for dim_index in range(1, 3):
        combined = apply_table(combined, dehier_table(extents[dim_index - 1]), dim_index)
    return (holding * combined)[None]


def solution(mesh):
    in_specs = (P("grid", "dom", None, None, None, None, None), P("grid", None), P("grid"))
    out_specs = P("grid", "dom", None, None, None, None, None)
    return jax.shard_map(body, mesh=mesh, in_specs=in_specs, out_specs=out_specs, check_vma=False)
```

profile of v0, /device:TPU:0, one launch (start us, length us, event | category | flops | bytes accessed | tf_op | source)
XLA Modules:
  0.0 215.0 jit_solution(8189721276518624149)
XLA Ops:
  6.5 1.6 copy-done
  8.1 5.0 %fusion.20 = f32[4,4,4,8,8,128]{5,1,4,3,2,0:T(4,128)S(1)} fusion(f32[4,4,1,1,1,1]{1,0,5,4,3,2:T(4,128)} %constant.141, f32[4,4,4,8,8,128]{5,4,3,2,1,0:T(8,128)S(1)} %bitcast.80), kind=kOutput, calls=%fused_computation.23 | convolution fusion | flops 25165824 | bytes 4194368 | tf_op jit(solution)/shard_map/abcdef,zb->azcdef/dot_general | solution.py:94
  13.2 0.0 copy-start.7
  13.2 4.3 %fusion.23 = f32[4,4,4,8,8,128]{5,2,4,3,1,0:T(4,128)S(1)} fusion(f32[4,4,1,1,1,1]{1,0,5,4,3,2:T(4,128)S(1)} %copy-done.9, f32[4,4,4,8,8,128]{5,1,4,3,2,0:T(4,128)S(1)} %fusion.20), kind=kOutput, calls=%fused_computation.24 | convolution fusion | flops 25165824 | bytes 4194368 | tf_op jit(solution)/shard_map/abcdef,zc->abzdef/dot_general | solution.py:94
  17.5 3.0 %fusion.26 = f32[4,4,4,8,8,128]{5,3,4,2,1,0:T(8,128)S(1)} fusion(f32[8,8,1,1,1,1]{1,0,5,4,3,2:T(8,128)S(1)} %copy-done.7, f32[4,4,4,8,8,128]{5,2,4,3,1,0:T(4,128)S(1)} %fusion.23), kind=kOutput, calls=%fused_computation.25 | convolution fusion | flops 50331648 | bytes 4194560 | tf_op jit(solution)/shard_map/abcdef,zd->abczef/dot_general | solution.py:94
  20.6 0.0 copy-start.3
  20.6 2.1 fusion.12
  22.7 0.0 copy-start.5
  22.7 1.9 fusion.4
  24.6 0.0 copy-start.1
  24.6 1.3 copy-done.1
  25.9 0.9 slice.110
  26.8 0.0 all-gather.3.cloned.1.call-update
  26.8 0.2 reduce-scatter.2.cloned.1.call-start
  27.1 0.7 fusion.39
  32.2 0.1 compare_convert_fusion.5
  32.4 0.2 multiply_multiply_fusion.2
  32.6 43.1 %all-gather.3.cloned.1.call-done = f32[4,4,4,8,8,128]{5,4,3,2,1,0:T(8,128)} async-done(((f32[1,4,4,8,8,128]{5,4,3,2,1,0:T(8,128)}), f32[4,4,4,8,8,128]{5,4,3,2,1,0:T(8,128)}) %all-gather.3.cloned.1.call-update) | async-done | bytes 2097168 | tf_op jit(solution)/shard_map/all_gather | solution.py:125
  75.6 6.4 %fusion.8 = f32[4,4,8,8,128,4]{4,5,3,2,1,0:T(4,128)S(1)} fusion(f32[4,4,1,1,1,1]{1,0,5,4,3,2:T(4,128)S(1)} %copy-done.13, f32[4,4,4,8,8,128]{5,4,3,2,1,0:T(8,128)} %all-gather.3.cloned.1.call-done), kind=kOutput, calls=%fused_computation.10 | convolution fusion | flops 25165824 | bytes 4194368 | tf_op jit(solution)/shard_map/abcdef,za->zbcdef/dot_general | solution.py:94
  82.1 0.0 copy-start.2
  82.1 0.0 copy-start.14
  82.1 0.6 dynamic-slice_bitcast_fusion
  82.7 1.1 dynamic-slice_bitcast_fusion.1
  83.8 5.4 %multiply_add_fusion = f32[4,4,4,8,8,128]{5,0,4,3,2,1:T(4,128)} fusion(f32[4,4,1,1,1,1]{1,0,5,4,3,2:T(4,128)S(1)} %copy-done.12, f32[4,4,4,8,8,128]{5,4,3,2,1,0:T(8,128)S(1)} %copy-done.2, f32[4,4,8,8,128]{4,3,2,1,0:T(8,128)S(1)} %dynamic-slice_bitcast_fusion.1, f32[4]{0:T(128)S(1)} %copy-done.14), kind=kOutput, calls=%fused_computation.22 | convolution fusion | flops 26214400 | bytes 4718672 | tf_op jit(solution)/shard_map/abcdef,za->zbcdef/dot_general | solution.py:94
  89.3 13.8 %scatter.6 = f32[4,4,4,8,8,128]{5,0,4,3,2,1:T(4,128)} dynamic-update-slice(f32[4,4,4,8,8,128]{5,0,4,3,2,1:T(4,128)} %multiply_add_fusion, f32[1,4,4,8,8,128]{5,0,4,3,2,1:T(1,128)S(1)} %dynamic-slice_bitcast_fusion, s32[]{:T(128)} %constant.120.clone.1, s32[]{:T(128)} %constant.120.clone.1, s32[]{:T(128)} %constant.120.clone.1, s32[]{:T(128)} %constant.120.clone.1, s32[]{:T(128)} %constant.120.clone.1, ...) | dynamic-update-slice | bytes 1048580 | tf_op jit(solution)/shard_map/scatter | solution.py:135
  103.1 2.3 %fusion = f32[4,4,4,8,8,128]{5,0,4,3,2,1:T(4,128)S(1)} fusion(f32[4,4,4,8,8,128]{5,0,4,3,2,1:T(4,128)} %scatter.6, f32[]{:T(128)} %bitcast.8, f32[4,4,8,8,128]{4,3,2,1,0:T(8,128)S(1)} %multiply_multiply_fusion.2, f32[4]{0:T(128)S(1)} %compare_convert_fusion.5), kind=kLoop, calls=%fused_computation.2 | loop fusion | flops 1572864 | bytes 4718612 | tf_op jit(solution)/shard_map/mul | solution.py:168
  105.4 1.6 copy.55
  107.1 0.0 copy-start.15
  107.1 0.0 reduce-scatter.2.cloned.1.call-update
  107.1 0.0 copy-start.8
  107.1 0.0 all-gather.5.cloned.1.call-start
  107.2 40.0 %reduce-scatter.2.cloned.1.call-done = f32[4,2,8,8,128]{4,3,2,0,1:T(8,128)} async-done(((f32[4,16,8,8,128]{4,3,2,0,1:T(8,128)}), f32[4,2,8,8,128]{4,3,2,0,1:T(8,128)}) %reduce-scatter.2.cloned.1.call-update) | async-done | bytes 262160 | tf_op jit(solution)/shard_map/reduce_scatter | solution.py:170
  147.2 1.3 convolution_bitcast_fusion.1
  148.5 0.4 convolution_bitcast_fusion
  148.9 0.4 fusion.40
  149.3 14.2 %all_gather.10 = f32[4,2,8,8,128]{4,3,2,1,0:T(8,128)S(1)} all-gather(f32[1,2,8,8,128]{4,3,2,1,0:T(8,128)S(1)} %slice.111), channel_id=1, replica_groups=mesh['grid'=8,'dom'=4] {'dom'}, dimensions={0}, use_global_device_ids=true | all-gather | bytes 327680 | tf_op jit(solution)/shard_map/all_gather | solution.py:142
  163.5 0.7 fusion.35
  164.2 0.1 constant_dynamic-slice_fusion
  164.4 0.0 copy-done.10
  164.4 0.0 copy-done.15
  164.4 0.7 convolution_add_fusion
  165.1 0.7 copy.60
  165.8 0.0 all-gather.5.cloned.1.call-update
  165.8 28.6 %all-gather.5.cloned.1.call-done = f32[4,16,8,8,128]{4,3,2,0,1:T(8,128)} async-done(((f32[4,2,8,8,128]{4,3,2,0,1:T(8,128)}), f32[4,16,8,8,128]{4,3,2,0,1:T(8,128)}) %all-gather.5.cloned.1.call-update) | async-done | bytes 2097168 | tf_op jit(solution)/shard_map/all_gather | solution.py:174
  194.4 6.4 %fusion.31 = f32[4,4,4,8,8,128]{5,1,4,3,2,0:T(4,128)S(1)} fusion(f32[4,4,1,1,1,1]{1,0,5,4,3,2:T(4,128)S(1)} %copy-done.8, f32[4,4,4,8,8,128]{5,4,3,0,2,1:T(8,128)} %bitcast.82), kind=kOutput, calls=%fused_computation.26 | convolution fusion | flops 25165824 | bytes 4194368 | tf_op jit(solution)/shard_map/abcdef,zb->azcdef/dot_general | solution.py:94
  200.9 4.3 %fusion.6 = f32[4,4,8,8,128,4]{4,5,3,2,1,0:T(4,128)S(1)} fusion(f32[4,4,1,1,1,1]{1,0,5,4,3,2:T(4,128)S(1)} %copy-done.8, f32[4,4,4,8,8,128]{5,1,4,3,2,0:T(4,128)S(1)} %fusion.31), kind=kOutput, calls=%fused_computation.8 | convolution fusion | flops 25165824 | bytes 4194368 | tf_op jit(solution)/shard_map/abcdef,zc->abzdef/dot_general | solution.py:94
  205.2 1.6 fusion.1
  206.9 1.6 copy.65
  (26 shorter events, 0.1 us)
Async XLA Ops:
  6.5 1.6 copy-start
  6.5 69.1 %all-gather.3.cloned.1.call-start = ((), (), s32[]{:S(2)}) async-start(), calls=%async_computation.1 | async-start | bytes 2621440 | tf_op jit(solution)/shard_map/all_gather | solution.py:125
  8.1 5.0 %copy-start.9 = (f32[4,4,1,1,1,1]{1,0,5,4,3,2:T(4,128)S(1)}, f32[4,4,1,1,1,1]{1,0,5,4,3,2:T(4,128)}, u32[]{:S(2)}) copy-start(f32[4,4,1,1,1,1]{1,0,5,4,3,2:T(4,128)} %constant.141) | copy-start | bytes 196
  13.2 4.4 %copy-start.7 = (f32[8,8,1,1,1,1]{1,0,5,4,3,2:T(8,128)S(1)}, f32[8,8,1,1,1,1]{1,0,5,4,3,2:T(8,128)}, u32[]{:S(2)}) copy-start(f32[8,8,1,1,1,1]{1,0,5,4,3,2:T(8,128)} %constant.142) | copy-start | bytes 772
  20.6 2.1 copy-start.3
  22.7 4.4 %copy-start.5 = (s32[1,6]{1,0:T(1,128)S(1)}, s32[1,6]{1,0:T(1,128)}, u32[]{:S(2)}) copy-start(s32[1,6]{1,0:T(1,128)} %param.24) | copy-start | bytes 76
  24.6 1.3 copy-start.1
  25.9 49.7 %copy-start.13 = (f32[4,4,1,1,1,1]{1,0,5,4,3,2:T(4,128)S(1)}, f32[4,4,1,1,1,1]{1,0,5,4,3,2:T(4,128)}, u32[]{:S(2)}) copy-start(f32[4,4,1,1,1,1]{1,0,5,4,3,2:T(4,128)} %constant.144) | copy-start | bytes 196
  26.8 120.4 %reduce-scatter.2.cloned.1.call-start = ((), (), s32[]{:S(2)}) async-start(), calls=%async_computation.2 | async-start | bytes 2359296 | tf_op jit(solution)/shard_map/reduce_scatter | solution.py:170
  75.6 8.2 %copy-start.12 = (f32[4,4,1,1,1,1]{1,0,5,4,3,2:T(4,128)S(1)}, f32[4,4,1,1,1,1]{1,0,5,4,3,2:T(4,128)}, u32[]{:S(2)}) copy-start(f32[4,4,1,1,1,1]{1,0,5,4,3,2:T(4,128)} %constant.140) | copy-start | bytes 196
  82.1 1.7 copy-start.2
  82.1 1.7 copy-start.14
  107.1 40.2 %copy-start.6 = (f32[8,8,1,1,1]{1,0,4,3,2:T(8,128)S(1)}, f32[8,8,1,1,1]{1,0,4,3,2:T(8,128)}, u32[]{:S(2)}) copy-start(f32[8,8,1,1,1]{1,0,4,3,2:T(8,128)} %constant.145) | copy-start | bytes 772
  107.1 41.8 %copy-start.4 = (f32[128,128,1,1,1]{1,0,4,3,2:T(8,128)S(1)}, f32[128,128,1,1,1]{1,0,4,3,2:T(8,128)}, u32[]{:S(2)}) copy-start(f32[128,128,1,1,1]{1,0,4,3,2:T(8,128)} %constant.146) | copy-start | bytes 196612
  107.1 56.4 %copy-start.11 = (f32[4,4,1,1,1]{1,0,4,3,2:T(4,128)S(1)}, f32[4,4,1,1,1]{1,0,4,3,2:T(4,128)}, u32[]{:S(2)}) copy-start(f32[4,4,1,1,1]{1,0,4,3,2:T(4,128)} %constant.147) | copy-start | bytes 196
  107.1 57.3 %copy-start.10 = (f32[4,4,1,1,1]{1,0,4,3,2:T(4,128)S(1)}, f32[4,4,1,1,1]{1,0,4,3,2:T(4,128)}, u32[]{:S(2)}) copy-start(f32[4,4,1,1,1]{1,0,4,3,2:T(4,128)} %constant.139) | copy-start | bytes 196
  107.1 57.3 %copy-start.15 = (f32[4]{0:T(128)S(1)}, f32[4]{0:T(128)}, u32[]{:S(2)}) copy-start(f32[4]{0:T(128)} %constant.134.clone) | copy-start | bytes 52
  107.1 87.3 %copy-start.8 = (f32[4,4,1,1,1,1]{1,0,5,4,3,2:T(4,128)S(1)}, f32[4,4,1,1,1,1]{1,0,5,4,3,2:T(4,128)}, u32[]{:S(2)}) copy-start(f32[4,4,1,1,1,1]{1,0,5,4,3,2:T(4,128)} %constant.148) | copy-start | bytes 196
  107.1 87.3 %all-gather.5.cloned.1.call-start = ((), (), s32[]{:S(2)}) async-start(), calls=%async_computation.3 | async-start | bytes 2359296 | tf_op jit(solution)/shard_map/all_gather | solution.py:174
Sparse Core Ops, SparseCore 0:
  26.9 48.6 all-gather.2
  107.2 39.9 reduce-scatter.1
  165.9 28.4 all-gather.4
where the time goes:
time: 216 us; the launch traced here: 215 us
  waiting for transfers between devices  112 us (52%)
  matrix products  42.5 us (20%)
  local copies, waits for them, and re-layouts  24.1 us (11%)
  between operations  17.9 us (8%)
  blocking collectives  14.2 us (7%)
  other arithmetic  4.28 us (2%)
    all_gather x1, waiting for transfers between devices, split_hierarchize(): all_firsts = lax.all_gather(first_row[None], 'dom', axis=0, tiled=True)  43.1 us
    dot_general x14, matrix products, apply_table(): jnp.einsum(formula, grid_data, jnp.asarray(matrix, dtype=jnp.float32), pr...  42.5 us
    reduce_scatter x1, waiting for transfers between devices, body(): lax.psum_scatter(merged, 'grid', scatter_dimension=1, tiled=True)  40 us
    all_gather x1, waiting for transfers between devices, body(): gathered = lax.all_gather(own_share, 'grid', axis=1, tiled=True)  28.6 us
    all_gather x1, blocking collectives, split_dehierarchize(): all_firsts = lax.all_gather(first_row[None], 'dom', axis=0, tiled=True)  14.2 us
    scatter x1, local copies, waits for them, and re-layouts, split_hierarchize(): return result.at[0].set(new_first)  13.8 us
  transfers between devices with their start and end apart: 3, of which 3 were waited for; matrix products, arithmetic and copies ran while one was open for 0% of the time, Pallas kernels for 0%

commit v1 on v0

v1 whole, which is shorter than its diff:
```python
import functools

import jax
import jax.numpy as jnp
import numpy as np
from jax import lax
from jax.experimental import pallas as pl
from jax.experimental.pallas import tpu as pltpu
from jax.sharding import PartitionSpec as P

MESH = pl.DeviceIdType.MESH


def coarse_position(numerator, level_now):
    while numerator > 0 and numerator % 2 == 0:
        numerator = numerator // 2
        level_now = level_now - 1
    if numerator == 0:
        return 0
    return (1 << level_now - 1) + (numerator - 1) // 2


def parent_positions(position):
    level_now = position.bit_length()
    span_size = 1 << level_now - 1
    offset = position - span_size
    return [
        coarse_position(offset % span_size, level_now - 1),
        coarse_position((offset + 1) % span_size, level_now - 1),
    ]


def hier_table(points):
    matrix = np.eye(points)
    for position in range(1, points):
        for parent in parent_positions(position):
            matrix[position, parent] -= 0.5
    return matrix


def dehier_table(points):
    matrix = np.zeros((points, points))
    matrix[0, 0] = 1.0
    for position in range(1, points):
        row_now = np.zeros(points)
        row_now[position] = 1.0
        for parent in parent_positions(position):
            row_now = row_now + 0.5 * matrix[parent]
        matrix[position] = row_now
    return matrix


def local_hier(points):
    matrix = np.zeros((points, points + 1))
    matrix[0, 0] = 1.0
    for point in range(1, points):
        stride = point & -point
        matrix[point, point] = 1.0
        matrix[point, point - stride] -= 0.5
        matrix[point, point + stride] -= 0.5
    return matrix


def local_dehier(points):
    matrix = np.zeros((points + 1, points + 1))
    matrix[0, 0] = 1.0
    matrix[points, points] = 1.0
    stride = points // 2
    while stride >= 1:
        for point in range(stride, points, 2 * stride):
            row_now = np.zeros(points + 1)
            row_now[point] = 1.0
            matrix[point] = row_now + 0.5 * (matrix[point - stride] + matrix[point + stride])
        stride = stride // 2
    return matrix[:points]


SHORTFALLS = 3


def projection_tables(points):
    top = points.bit_length() - 1
    hier, dehier = hier_table(points), dehier_table(points)
    return [
        dehier @ np.diag((np.arange(points) < (1 << max(top - s, 0))).astype(np.float64)) @ hier
        for s in range(SHORTFALLS)
    ]


def row_tables(points):
    last = np.zeros((1, points + 1))
    last[0, points] = 1.0
    hier = np.concatenate([local_hier(points), last])
    result = []
    for s in range(SHORTFALLS):
        held = (np.arange(points + 1) % (1 << s) == 0).astype(np.float64)
        held[points] = 1.0
        result.append(local_dehier(points) @ np.diag(held) @ hier)
    return np.stack(result)


def holding_mask(level_row, extents):
    holding = jnp.ones(extents, dtype=jnp.float32)
    for dim_index, points in enumerate(extents):
        limit = jnp.left_shift(jnp.int32(1), level_row[dim_index])
        inside = (jnp.arange(points, dtype=jnp.int32) < limit).astype(jnp.float32)
        shape_now = [1] * len(extents)
        shape_now[dim_index] = points
        holding = holding * inside.reshape(shape_now)
    return holding


def split_rows_mask(level_count, local_rows, rank_count):
    members = lax.axis_size("dom")
    total_rows = local_rows * members
    rows_here = lax.axis_index("dom") * local_rows + jnp.arange(local_rows, dtype=jnp.int32)
    spacing = jnp.right_shift(jnp.int32(total_rows), level_count)
    inside = (jnp.remainder(rows_here, spacing) == 0).astype(jnp.float32)
    return inside.reshape((local_rows,) + (1,) * (rank_count - 1))


def split_dot(data, right=None, left=None):
    high = data.astype(jnp.bfloat16)
    low = (data - high.astype(jnp.float32)).astype(jnp.bfloat16)
    if right is not None:
        return jnp.dot(high, right, preferred_element_type=jnp.float32) + jnp.dot(
            low, right, preferred_element_type=jnp.float32
        )
    return jnp.dot(left, high, preferred_element_type=jnp.float32) + jnp.dot(
        left, low, preferred_element_type=jnp.float32
    )


def kernel(groups, members, v_ref, inner_ref, lane_ref, outer_ref, row_ref, out_ref,
           follow, part, acc, recv, send_sem, recv_sem, z_send, z_recv):
    rows, depth, lanes = v_ref.shape
    steps = groups.bit_length() - 1
    me = lax.axis_index("grid")
    dom = lax.axis_index("dom")
    core = lax.rem(me, 2)
    before = lax.rem(dom + members - 1, members)
    after = lax.rem(dom + 1, members)

    bits, partners = [], []
    for step in range(steps):
        up = 1 << step
        down = 1 << (steps - step) if step else 1
        bit_up = lax.rem(me // up, 2)
        bit_down = lax.rem(me // down, 2)
        bit = bit_up + core * (bit_down - bit_up)
        stride = up + core * (down - up)
        bits.append(bit)
        partners.append(me + (1 - 2 * bit) * stride)

    barrier = pltpu.get_barrier_semaphore()
    for partner in partners:
        pl.semaphore_signal(barrier, inc=1, device_id={"grid": partner}, device_id_type=MESH)
    for near in (before, after):
        pl.semaphore_signal(barrier, inc=1, device_id={"dom": near}, device_id_type=MESH)
    pl.semaphore_wait(barrier, steps + 2)

    shift = pltpu.make_async_remote_copy(
        src_ref=v_ref.at[0], dst_ref=follow, send_sem=z_send, recv_sem=z_recv,
        device_id={"dom": before}, device_id_type=MESH,
    )
    shift.start()

    outer = outer_ref.shape[0]
    span = depth // outer

    def project(data):
        blocks = [split_dot(data[i * span : (i + 1) * span], left=inner_ref[...]) for i in range(outer)]
        mixed = []
        for i in range(outer):
            total = outer_ref[i, 0] * blocks[0]
            for j in range(1, outer):
                total = total + outer_ref[i, j] * blocks[j]
            mixed.append(total)
        return split_dot(jnp.concatenate(mixed, axis=0), right=lane_ref[...])

    def reduce_chunk(index, start, size):
        low, now = start, size
        lows = [low]
        taken = start
        for step in range(steps):
            half = now // 2
            keep = pl.multiple_of(low + bits[step] * half, 8)
            give = pl.multiple_of(low + (1 - bits[step]) * half, 8)
            copy = pltpu.make_async_remote_copy(
                src_ref=acc.at[pl.ds(give, half)], dst_ref=recv.at[pl.ds(taken, half)],
                send_sem=send_sem.at[index, step], recv_sem=recv_sem.at[index, step],
                device_id={"grid": partners[step]}, device_id_type=MESH,
            )
            copy.start()
            yield
            copy.wait()
            total = acc[pl.ds(keep, half), :] + recv[taken : taken + half, :]
            if step == steps - 1:
                out_ref[pl.ds(keep, half), :] = total
            else:
                acc[pl.ds(keep, half), :] = total
            taken += half
            low, now = keep, half
            lows.append(low)
        for step in range(steps - 1, -1, -1):
            mine = out_ref.at[pl.ds(lows[step + 1], now)]
            copy = pltpu.make_async_remote_copy(
                src_ref=mine, dst_ref=mine,
                send_sem=send_sem.at[index, 2 * steps - 1 - step],
                recv_sem=recv_sem.at[index, 2 * steps - 1 - step],
                device_id={"grid": partners[step]}, device_id_type=MESH,
            )
            copy.start()
            yield
            copy.wait()
            now *= 2

    first = project(v_ref[0])
    part[0] = first
    acc[0:depth, :] = row_ref[0, 0] * first
    head = reduce_chunk(0, 0, depth)
    next(head)
    for row in range(1, rows):
        part[row] = project(v_ref[row])
    next(head)
    shift.wait()
    part[rows] = project(follow[...])
    for row in range(1, rows):
        total = row_ref[row, 0] * part[0]
        for source in range(1, rows + 1):
            total = total + row_ref[row, source] * part[source]
        acc[row * depth : (row + 1) * depth, :] = total
    active = [reduce_chunk(1, depth, (rows - 1) * depth), head]
    while active:
        active = [chunk for chunk in active if next(chunk, "end") != "end"]


def body(values, levels, coefficients):
    grid_data = values[0]
    level_row = levels[0]
    weight = coefficients[0].astype(jnp.float32)
    local_rows = grid_data.shape[0]
    extents = tuple(grid_data.shape[1:])
    groups, members = lax.axis_size("grid"), lax.axis_size("dom")
    lanes = extents[-1]
    depth = int(np.prod(extents[:-1]))
    span = depth // extents[0]

    tops = [local_rows * members] + list(extents)
    short = jnp.asarray([t.bit_length() - 1 for t in tops], jnp.int32) - level_row
    third, fourth, fifth = (projection_tables(points) for points in extents[1:4])
    combos = [(i, j, k) for i in range(SHORTFALLS) for j in range(SHORTFALLS) for k in range(SHORTFALLS)
              if i + j + k < SHORTFALLS]
    place = np.zeros((SHORTFALLS,) * 3, np.int32)
    for at, combo in enumerate(combos):
        place[combo] = at
    inner_all = np.stack([np.kron(np.kron(third[i], fourth[j]), fifth[k]) for i, j, k in combos])
    which = jnp.asarray(place)[short[2], short[3], short[4]]
    inner = lax.dynamic_index_in_dim(jnp.asarray(inner_all, jnp.bfloat16), which, 0, keepdims=False)
    lane = lax.dynamic_index_in_dim(
        jnp.asarray(np.stack(projection_tables(lanes)).transpose(0, 2, 1), jnp.bfloat16), short[5], 0, keepdims=False)
    outer = jnp.asarray(np.stack(projection_tables(extents[0])), jnp.float32)[short[1]]
    rows = jnp.asarray(row_tables(local_rows), jnp.float32)[short[0]] * weight

    steps = groups.bit_length() - 1
    vmem = pl.BlockSpec(memory_space=pltpu.VMEM)
    smem = pl.BlockSpec(memory_space=pltpu.SMEM)
    combined = pl.pallas_call(
        functools.partial(kernel, groups, members),
        out_shape=jax.ShapeDtypeStruct((local_rows * depth, lanes), jnp.float32),
        in_specs=[vmem, vmem, vmem, smem, smem],
        out_specs=vmem,
        scratch_shapes=[
            pltpu.VMEM((depth, lanes), jnp.float32),
            pltpu.VMEM((local_rows + 1, depth, lanes), jnp.float32),
            pltpu.VMEM((local_rows * depth, lanes), jnp.float32),
            pltpu.VMEM((local_rows * depth, lanes), jnp.float32),
            pltpu.SemaphoreType.DMA((2, 2 * steps)),
            pltpu.SemaphoreType.DMA((2, 2 * steps)),
            pltpu.SemaphoreType.DMA,
            pltpu.SemaphoreType.DMA,
        ],
        compiler_params=pltpu.CompilerParams(
            collective_id=0, has_side_effects=True, vmem_limit_bytes=40 * 1024 * 1024
        ),
    )(grid_data.reshape(local_rows, depth, lanes), inner, lane, outer, rows)
    holding = (
        split_rows_mask(level_row[0], local_rows, grid_data.ndim)
        * holding_mask(level_row[1:], extents)[None]
    )
    return (holding * combined.reshape(grid_data.shape))[None]


def solution(mesh):
    in_specs = (P("grid", "dom", None, None, None, None, None), P("grid", None), P("grid"))
    out_specs = P("grid", "dom", None, None, None, None, None)
    return jax.shard_map(body, mesh=mesh, in_specs=in_specs, out_specs=out_specs, check_vma=False)
```

time: 216 us -> 75.6 us (0.35)
  waiting for transfers between devices: 112 us -> 0 us
  Pallas kernels: 0 us -> 46.9 us
  matrix products: 42.5 us -> 0 us
  local copies, waits for them, and re-layouts: 24.1 us -> 7.42 us
  blocking collectives: 14.2 us -> 0 us
    all_gather x2 -> x0, waiting for transfers between devices: 71.7 us -> none  [the longest x1 43.1 us: split_hierarchize(): all_firsts = lax.all_gather(first_row[None], 'dom', axis=0, tiled=True)]
    pallas_call x0 -> x1, Pallas kernels: none -> 46.9 us  [body(): pl.pallas_call(functools.partial(kernel, groups, members), out_shape=jax....]
    dot_general x14 -> x0, matrix products: 42.5 us -> none  [apply_table(): jnp.einsum(formula, grid_data, jnp.asarray(matrix, dtype=jnp.float32), pr...]
    reduce_scatter x1 -> x0, waiting for transfers between devices: 40 us -> none  [body(): lax.psum_scatter(merged, 'grid', scatter_dimension=1, tiled=True)]
    all_gather x1 -> x0, blocking collectives: 14.2 us -> none  [split_dehierarchize(): all_firsts = lax.all_gather(first_row[None], 'dom', axis=0, tiled=True)]
    scatter x2 -> x0, local copies, waits for them, and re-layouts: 13.8 us -> none  [the longest x1 13.8 us: split_hierarchize(): return result.at[0].set(new_first)]
    squeeze x0 -> x3, local copies, waits for them, and re-layouts: none -> 2.36 us  [the longest x1 0.91 us: body(): lax.dynamic_index_in_dim(jnp.asarray(inner_all, jnp.bfloat16), which, 0,...]
  transfers between devices with their start and end apart: 3 -> 0, of which waited for: 3 -> 0; matrix products, arithmetic and copies ran while one was open for 0% -> 0% of each run, Pallas kernels for 0% -> 0%
where the time goes in v1:
time: 75.6 us; the launch traced here: 75 us
  Pallas kernels  46.9 us (62%)
  between operations  17.4 us (23%)
  local copies, waits for them, and re-layouts  7.42 us (10%)
  other arithmetic  3.35 us (4%)
    pallas_call x1, Pallas kernels, body(): pl.pallas_call(functools.partial(kernel, groups, members), out_shape=jax....  46.9 us
    mul x1, other arithmetic, body(): return (holding * combined.reshape(grid_data.shape))[None]  1.65 us
    unnamed x2, local copies, waits for them, and re-layouts  1.59 us
    slice x1, local copies, waits for them, and re-layouts, body(): level_row[0]  1.53 us

profile of v1, /device:TPU:0, one launch (start us, length us, event | category | flops | bytes accessed | tf_op | source)
XLA Modules:
  0.0 75.0 jit_solution(16310526348596673208)
XLA Ops:
  0.7 0.7 sub.4
  1.3 0.7 fusion.1
  7.6 1.3 %dynamic_slice.17 = s32[1,1,1]{2,1,0:T(1,128)} dynamic-slice(s32[3,3,3]{2,1,0:T(4,128)} %constant.50.clone, s32[]{:T(128)S(6)} %select_n.38, s32[]{:T(128)S(6)} %select_n.39, s32[]{:T(128)S(6)} %select_n.40), dynamic_slice_sizes={1,1,1} | dynamic-slice | bytes 12 | tf_op jit(solution)/shard_map/dynamic_slice | solution.py:258
  16.2 0.7 multiply_bitcast_fusion.row_ref
  16.9 0.7 dynamic-slice_bitcast_fusion.2.outer_ref
  17.6 1.5 %fusion = (s32[1,1]{1,0:T(1,128)}, s32[1,1]{1,0:T(1,128)}, s32[1,1]{1,0:T(1,128)}, s32[1,1]{1,0:T(1,128)}, s32[1,1]{1,0:T(1,128)}, /*index=5*/s32[1,1]{1,0:T(1,128)}) fusion(s32[1,6]{1,0:T(1,128)} %param.10), kind=kLoop, calls=%fused_computation.13 | loop fusion | bytes 48 | tf_op jit(solution)/shard_map/slice | solution.py:288
  22.8 0.1 compare_convert_fusion.5
  23.0 0.8 %dynamic-slice_bitcast_fusion.1.lane_ref = bf16[128,128]{1,0:T(8,128)(2,1)S(1)} fusion(bf16[3,128,128]{2,1,0:T(8,128)(2,1)} %constant.52.clone, s32[]{:T(128)S(6)} %select_n.42), kind=kLoop, calls=%fused_computation.3 | loop fusion | bytes 65540 | tf_op jit(solution)/shard_map/jit(dynamic_index_in_dim)/squeeze | solution.py:260
  23.8 0.9 %dynamic-slice_bitcast_fusion.inner_ref = bf16[256,256]{1,0:T(8,128)(2,1)S(1)} fusion(bf16[10,256,256]{2,1,0:T(8,128)(2,1)} %constant.51.clone, s32[]{:T(128)S(6)} %select_n.41), kind=kLoop, calls=%fused_computation.2 | loop fusion | bytes 262148 | tf_op jit(solution)/shard_map/jit(dynamic_index_in_dim)/squeeze | solution.py:259
  24.7 0.2 multiply_multiply_fusion.1
  24.9 0.0 copy-start
  24.9 1.6 %copy-done = f32[1,4,4,4,8,8,128]{6,5,4,3,2,1,0:T(8,128)S(1)} copy-done((f32[1,4,4,4,8,8,128]{6,5,4,3,2,1,0:T(8,128)S(1)}, f32[1,4,4,4,8,8,128]{6,5,4,3,2,1,0:T(8,128)}, u32[]{:S(2)}) %copy-start) | copy-done | bytes 2097176
  26.5 46.9 %shard_map.91 = f32[4096,128]{1,0:T(8,128)S(1)} custom-call(f32[4,1024,128]{2,1,0:T(8,128)S(1)} %bitcast.25, bf16[256,256]{1,0:T(8,128)(2,1)S(1)} %dynamic-slice_bitcast_fusion.inner_ref, bf16[128,128]{1,0:T(8,128)(2,1)S(1)} %dynamic-slice_bitcast_fusion.1.lane_ref, f32[4,4]{1,0:T(4,128)S(1)} %dynamic-slice_bitcast_fusion.2.outer_ref, ...), custom_call_target="tpu_custom_call" | custom-call | tf_op jit(solution)/shard_map/pallas_call | solution.py:268
  73.4 1.7 %multiply_multiply_fusion = f32[1,4,4,4,8,8,128]{6,5,4,3,2,1,0:T(8,128)} fusion(f32[1,4,4,4,8,8,128]{6,5,4,3,2,1,0:T(8,128)S(1)} %bitcast.24, f32[4,4,8,8,128]{4,3,2,1,0:T(8,128)S(1)} %multiply_multiply_fusion.1, f32[4]{0:T(128)S(1)} %compare_convert_fusion.5), kind=kLoop, calls=%fused_computation | loop fusion | flops 1048576 | bytes 4718608 | tf_op jit(solution)/shard_map/mul | solution.py:291
  (3 shorter events, 0.0 us)
Async XLA Ops:
  24.9 1.6 %copy-start = (f32[1,4,4,4,8,8,128]{6,5,4,3,2,1,0:T(8,128)S(1)}, f32[1,4,4,4,8,8,128]{6,5,4,3,2,1,0:T(8,128)}, u32[]{:S(2)}) copy-start(f32[1,4,4,4,8,8,128]{6,5,4,3,2,1,0:T(8,128)} %param.9) | copy-start | bytes 6291460

commit v2 on v1

--- a/solution.py
+++ b/solution.py
@@ -131,7 +131,16 @@
     )
 
 
-def kernel(groups, members, v_ref, inner_ref, lane_ref, outer_ref, row_ref, out_ref,
+def pick(tables, short):
+    return [
+        [jnp.where(short == 0, float(tables[0][i][j]),
+                   jnp.where(short == 1, float(tables[1][i][j]), float(tables[2][i][j])))
+         for j in range(len(tables[0][0]))]
+        for i in range(len(tables[0]))
+    ]
+
+
+def kernel(groups, members, tops, v_ref, level_ref, weight_ref, inner_ref, lane_ref, out_ref,
            follow, part, acc, recv, send_sem, recv_sem, z_send, z_recv):
     rows, depth, lanes = v_ref.shape
     steps = groups.bit_length() - 1
@@ -152,6 +161,10 @@
         bits.append(bit)
         partners.append(me + (1 - 2 * bit) * stride)
 
+    short = [
+        jnp.clip(top.bit_length() - 1 - level_ref[0, k], 0, SHORTFALLS - 1) for k, top in enumerate(tops)
+    ]
+
     barrier = pltpu.get_barrier_semaphore()
     for partner in partners:
         pl.semaphore_signal(barrier, inc=1, device_id={"grid": partner}, device_id_type=MESH)
@@ -165,18 +178,24 @@
     )
     shift.start()
 
-    outer = outer_ref.shape[0]
+    outer = tops[1]
     span = depth // outer
+    outer_at = pick(projection_tables(outer), short[1])
+    row_at = pick(row_tables(rows), short[0])
+    weight = weight_ref[0].astype(jnp.float32)
+    row_at = [[weight * entry for entry in line] for line in row_at]
+    inner = inner_ref[short[2]] * inner_ref[SHORTFALLS + short[3]] * inner_ref[2 * SHORTFALLS + short[4]]
+    lane = lane_ref[short[5]]
 
     def project(data):
-        blocks = [split_dot(data[i * span : (i + 1) * span], left=inner_ref[...]) for i in range(outer)]
+        blocks = [split_dot(data[i * span : (i + 1) * span], left=inner) for i in range(outer)]
         mixed = []
         for i in range(outer):
-            total = outer_ref[i, 0] * blocks[0]
+            total = outer_at[i][0] * blocks[0]
             for j in range(1, outer):
-                total = total + outer_ref[i, j] * blocks[j]
+                total = total + outer_at[i][j] * blocks[j]
             mixed.append(total)
-        return split_dot(jnp.concatenate(mixed, axis=0), right=lane_ref[...])
+        return split_dot(jnp.concatenate(mixed, axis=0), right=lane)
 
     def reduce_chunk(index, start, size):
         low, now = start, size
@@ -217,7 +236,7 @@
 
     first = project(v_ref[0])
     part[0] = first
-    acc[0:depth, :] = row_ref[0, 0] * first
+    acc[0:depth, :] = row_at[0][0] * first
     head = reduce_chunk(0, 0, depth)
     next(head)
     for row in range(1, rows):
@@ -225,12 +244,15 @@
     next(head)
     shift.wait()
     part[rows] = project(follow[...])
+    active = [head]
     for row in range(1, rows):
-        total = row_ref[row, 0] * part[0]
+        total = row_at[row][0] * part[0]
         for source in range(1, rows + 1):
-            total = total + row_ref[row, source] * part[source]
+            total = total + row_at[row][source] * part[source]
         acc[row * depth : (row + 1) * depth, :] = total
-    active = [reduce_chunk(1, depth, (rows - 1) * depth), head]
+        chunk = reduce_chunk(row, row * depth, depth)
+        next(chunk)
+        active.append(chunk)
     while active:
         active = [chunk for chunk in active if next(chunk, "end") != "end"]
 
@@ -238,52 +260,44 @@
 def body(values, levels, coefficients):
     grid_data = values[0]
     level_row = levels[0]
-    weight = coefficients[0].astype(jnp.float32)
     local_rows = grid_data.shape[0]
     extents = tuple(grid_data.shape[1:])
     groups, members = lax.axis_size("grid"), lax.axis_size("dom")
     lanes = extents[-1]
     depth = int(np.prod(extents[:-1]))
-    span = depth // extents[0]
 
     tops = [local_rows * members] + list(extents)
-    short = jnp.asarray([t.bit_length() - 1 for t in tops], jnp.int32) - level_row
-    third, fourth, fifth = (projection_tables(points) for points in extents[1:4])
-    combos = [(i, j, k) for i in range(SHORTFALLS) for j in range(SHORTFALLS) for k in range(SHORTFALLS)
-              if i + j + k < SHORTFALLS]
-    place = np.zeros((SHORTFALLS,) * 3, np.int32)
-    for at, combo in enumerate(combos):
-        place[combo] = at
-    inner_all = np.stack([np.kron(np.kron(third[i], fourth[j]), fifth[k]) for i, j, k in combos])
-    which = jnp.asarray(place)[short[2], short[3], short[4]]
-    inner = lax.dynamic_index_in_dim(jnp.asarray(inner_all, jnp.bfloat16), which, 0, keepdims=False)
-    lane = lax.dynamic_index_in_dim(
-        jnp.asarray(np.stack(projection_tables(lanes)).transpose(0, 2, 1), jnp.bfloat16), short[5], 0, keepdims=False)
-    outer = jnp.asarray(np.stack(projection_tables(extents[0])), jnp.float32)[short[1]]
-    rows = jnp.asarray(row_tables(local_rows), jnp.float32)[short[0]] * weight
+    ones = [np.ones((points, points)) for points in extents[1:4]]
+    inner = []
+    for at, points in enumerate(extents[1:4]):
+        for table in projection_tables(points):
+            factors = ones[:at] + [table] + ones[at + 1 :]
+            inner.append(np.kron(np.kron(factors[0], factors[1]), factors[2]))
+    inner = jnp.asarray(np.stack(inner), jnp.bfloat16)
+    lane = jnp.asarray(np.stack(projection_tables(lanes)).transpose(0, 2, 1), jnp.bfloat16)
 
     steps = groups.bit_length() - 1
     vmem = pl.BlockSpec(memory_space=pltpu.VMEM)
     smem = pl.BlockSpec(memory_space=pltpu.SMEM)
     combined = pl.pallas_call(
-        functools.partial(kernel, groups, members),
+        functools.partial(kernel, groups, members, tops),
         out_shape=jax.ShapeDtypeStruct((local_rows * depth, lanes), jnp.float32),
-        in_specs=[vmem, vmem, vmem, smem, smem],
+        in_specs=[vmem, smem, smem, vmem, vmem],
         out_specs=vmem,
         scratch_shapes=[
             pltpu.VMEM((depth, lanes), jnp.float32),
             pltpu.VMEM((local_rows + 1, depth, lanes), jnp.float32),
             pltpu.VMEM((local_rows * depth, lanes), jnp.float32),
             pltpu.VMEM((local_rows * depth, lanes), jnp.float32),
-            pltpu.SemaphoreType.DMA((2, 2 * steps)),
-            pltpu.SemaphoreType.DMA((2, 2 * steps)),
+            pltpu.SemaphoreType.DMA((local_rows, 2 * steps)),
+            pltpu.SemaphoreType.DMA((local_rows, 2 * steps)),
             pltpu.SemaphoreType.DMA,
             pltpu.SemaphoreType.DMA,
         ],
         compiler_params=pltpu.CompilerParams(
             collective_id=0, has_side_effects=True, vmem_limit_bytes=40 * 1024 * 1024
         ),
-    )(grid_data.reshape(local_rows, depth, lanes), inner, lane, outer, rows)
+    )(grid_data.reshape(local_rows, depth, lanes), levels, coefficients, inner, lane)
     holding = (
         split_rows_mask(level_row[0], local_rows, grid_data.ndim)
         * holding_mask(level_row[1:], extents)[None]

time: 75.6 us -> 54 us (0.71)
  between operations: 17.4 us -> 4.49 us
  Pallas kernels: 46.9 us -> 41 us
  local copies, waits for them, and re-layouts: 7.42 us -> 5.96 us
  other arithmetic: 3.35 us -> 1.98 us
    pallas_call x1, Pallas kernels: 46.9 us -> 41 us  [body(): pl.pallas_call(functools.partial(kernel, groups, members, tops), out_shap...]
    unnamed x2 -> x8, local copies, waits for them, and re-layouts: 1.59 us -> 4.4 us
    squeeze x3 -> x0, local copies, waits for them, and re-layouts: 2.36 us -> none  [the longest x1 0.91 us: body(): lax.dynamic_index_in_dim(jnp.asarray(inner_all, jnp.bfloat16), which, 0,...]
    dynamic_slice x1 -> x0, local copies, waits for them, and re-layouts: 1.27 us -> none  [body(): which = jnp.asarray(place)[short[2], short[3], short[4]]]
where the time goes in v2:
time: 54 us; the launch traced here: 53.5 us
  Pallas kernels  41 us (76%)
  local copies, waits for them, and re-layouts  5.96 us (11%)
  between operations  4.49 us (8%)
  other arithmetic  1.98 us (4%)
    pallas_call x1, Pallas kernels, body(): pl.pallas_call(functools.partial(kernel, groups, members, tops), out_shap...  41 us
    unnamed x8, local copies, waits for them, and re-layouts  4.4 us
    mul x1, other arithmetic, body(): return (holding * combined.reshape(grid_data.shape))[None]  1.66 us
    slice x1, local copies, waits for them, and re-layouts, body(): level_row[0]  1.56 us

profile of v2, /device:TPU:0, one launch (start us, length us, event | category | flops | bytes accessed | tf_op | source)
XLA Modules:
  0.0 53.5 jit_solution(6529892102683115857)
XLA Ops:
  0.7 1.6 %fusion = (s32[1,1]{1,0:T(1,128)}, s32[1,1]{1,0:T(1,128)}, s32[1,1]{1,0:T(1,128)}, s32[1,1]{1,0:T(1,128)}, s32[1,1]{1,0:T(1,128)}, /*index=5*/s32[1,1]{1,0:T(1,128)}) fusion(s32[1,6]{1,0:T(1,128)} %level_ref.1), kind=kLoop, calls=%fused_computation.9 | loop fusion | bytes 48 | tf_op jit(solution)/shard_map/slice | solution.py:302
  6.0 0.1 compare_convert_fusion.5
  6.2 0.2 multiply_multiply_fusion.1
  6.4 0.0 copy-start
  6.4 1.6 %copy-done = f32[1,4,4,4,8,8,128]{6,5,4,3,2,1,0:T(8,128)S(1)} copy-done((f32[1,4,4,4,8,8,128]{6,5,4,3,2,1,0:T(8,128)S(1)}, f32[1,4,4,4,8,8,128]{6,5,4,3,2,1,0:T(8,128)}, u32[]{:S(2)}) %copy-start) | copy-done | bytes 2097176
  7.9 0.0 copy-start.1
  8.0 1.3 %copy-done.1 = bf16[9,256,256]{2,1,0:T(8,128)(2,1)S(1)} copy-done((bf16[9,256,256]{2,1,0:T(8,128)(2,1)S(1)}, bf16[9,256,256]{2,1,0:T(8,128)(2,1)}, u32[]{:S(2)}) %copy-start.1) | copy-done | bytes 1179672
  9.2 0.0 copy-start.2
  9.2 0.9 %copy-done.2 = bf16[3,128,128]{2,1,0:T(8,128)(2,1)S(1)} copy-done((bf16[3,128,128]{2,1,0:T(8,128)(2,1)S(1)}, bf16[3,128,128]{2,1,0:T(8,128)(2,1)}, u32[]{:S(2)}) %copy-start.2) | copy-done | bytes 98328
  10.1 0.0 copy-start.3
  10.1 0.7 %copy-done.3 = s32[1,6]{1,0:T(1,128)S(1)} copy-done((s32[1,6]{1,0:T(1,128)S(1)}, s32[1,6]{1,0:T(1,128)}, u32[]{:S(2)}) %copy-start.3) | copy-done | bytes 48
  10.8 41.0 %shard_map.55 = f32[4096,128]{1,0:T(8,128)S(1)} custom-call(f32[4,1024,128]{2,1,0:T(8,128)S(1)} %bitcast.9, s32[1,6]{1,0:T(1,128)S(1)} %copy-done.3, s32[1]{0:T(128)S(6)} %copy.6.weight_ref, bf16[9,256,256]{2,1,0:T(8,128)(2,1)S(1)} %copy-done.1, bf16[3,128,128]{2,1,0:T(8,128)(2,1)S(1)} %copy-done.2), custom_call_target="tpu_custom_call" | custom-call | tf_op jit(solution)/shard_map/pallas_call | solution.py:282
  51.8 1.7 %multiply_multiply_fusion = f32[1,4,4,4,8,8,128]{6,5,4,3,2,1,0:T(8,128)} fusion(f32[1,4,4,4,8,8,128]{6,5,4,3,2,1,0:T(8,128)S(1)} %bitcast.8, f32[4,4,8,8,128]{4,3,2,1,0:T(8,128)S(1)} %multiply_multiply_fusion.1, f32[4]{0:T(128)S(1)} %compare_convert_fusion.5), kind=kLoop, calls=%fused_computation | loop fusion | flops 1048576 | bytes 4718608 | tf_op jit(solution)/shard_map/mul | solution.py:305
  (3 shorter events, 0.0 us)
Async XLA Ops:
  6.4 1.6 %copy-start = (f32[1,4,4,4,8,8,128]{6,5,4,3,2,1,0:T(8,128)S(1)}, f32[1,4,4,4,8,8,128]{6,5,4,3,2,1,0:T(8,128)}, u32[]{:S(2)}) copy-start(f32[1,4,4,4,8,8,128]{6,5,4,3,2,1,0:T(8,128)} %param.5) | copy-start | bytes 6291460
  7.9 1.3 %copy-start.1 = (bf16[9,256,256]{2,1,0:T(8,128)(2,1)S(1)}, bf16[9,256,256]{2,1,0:T(8,128)(2,1)}, u32[]{:S(2)}) copy-start(bf16[9,256,256]{2,1,0:T(8,128)(2,1)} %constant.29.clone.inner_ref) | copy-start | bytes 3538948
  9.2 0.9 %copy-start.2 = (bf16[3,128,128]{2,1,0:T(8,128)(2,1)S(1)}, bf16[3,128,128]{2,1,0:T(8,128)(2,1)}, u32[]{:S(2)}) copy-start(bf16[3,128,128]{2,1,0:T(8,128)(2,1)} %constant.30.clone.lane_ref) | copy-start | bytes 294916
  10.1 0.7 %copy-start.3 = (s32[1,6]{1,0:T(1,128)S(1)}, s32[1,6]{1,0:T(1,128)}, u32[]{:S(2)}) copy-start(s32[1,6]{1,0:T(1,128)} %level_ref.1) | copy-start | bytes 76

commit v3 on v2

--- a/solution.py
+++ b/solution.py
@@ -99,26 +99,6 @@
     return np.stack(result)
 
 
-def holding_mask(level_row, extents):
-    holding = jnp.ones(extents, dtype=jnp.float32)
-    for dim_index, points in enumerate(extents):
-        limit = jnp.left_shift(jnp.int32(1), level_row[dim_index])
-        inside = (jnp.arange(points, dtype=jnp.int32) < limit).astype(jnp.float32)
-        shape_now = [1] * len(extents)
-        shape_now[dim_index] = points
-        holding = holding * inside.reshape(shape_now)
-    return holding
-
-
-def split_rows_mask(level_count, local_rows, rank_count):
-    members = lax.axis_size("dom")
-    total_rows = local_rows * members
-    rows_here = lax.axis_index("dom") * local_rows + jnp.arange(local_rows, dtype=jnp.int32)
-    spacing = jnp.right_shift(jnp.int32(total_rows), level_count)
-    inside = (jnp.remainder(rows_here, spacing) == 0).astype(jnp.float32)
-    return inside.reshape((local_rows,) + (1,) * (rank_count - 1))
-
-
 def split_dot(data, right=None, left=None):
     high = data.astype(jnp.bfloat16)
     low = (data - high.astype(jnp.float32)).astype(jnp.bfloat16)
@@ -141,7 +121,7 @@
 
 
 def kernel(groups, members, tops, v_ref, level_ref, weight_ref, inner_ref, lane_ref, out_ref,
-           follow, part, acc, recv, send_sem, recv_sem, z_send, z_recv):
+           follow, part, acc, recv, gathered, send_sem, recv_sem, z_send, z_recv):
     rows, depth, lanes = v_ref.shape
     steps = groups.bit_length() - 1
     me = lax.axis_index("grid")
@@ -215,14 +195,14 @@
             copy.wait()
             total = acc[pl.ds(keep, half), :] + recv[taken : taken + half, :]
             if step == steps - 1:
-                out_ref[pl.ds(keep, half), :] = total
+                gathered[pl.ds(keep, half), :] = total
             else:
                 acc[pl.ds(keep, half), :] = total
             taken += half
             low, now = keep, half
             lows.append(low)
         for step in range(steps - 1, -1, -1):
-            mine = out_ref.at[pl.ds(lows[step + 1], now)]
+            mine = gathered.at[pl.ds(lows[step + 1], now)]
             copy = pltpu.make_async_remote_copy(
                 src_ref=mine, dst_ref=mine,
                 send_sem=send_sem.at[index, 2 * steps - 1 - step],
@@ -233,6 +213,14 @@
             yield
             copy.wait()
             now *= 2
+
+    place = lax.broadcasted_iota(jnp.int32, (depth, lanes), 0)
+    inside = lax.broadcasted_iota(jnp.int32, (depth, lanes), 1) < (lanes >> short[5])
+    below = depth
+    for k in range(1, 5):
+        below //= tops[k]
+        inside &= ((place // below) % tops[k]) < (tops[k] >> short[k])
+    held = inside.astype(jnp.float32)
 
     first = project(v_ref[0])
     part[0] = first
@@ -255,6 +243,9 @@
         active.append(chunk)
     while active:
         active = [chunk for chunk in active if next(chunk, "end") != "end"]
+    for row in range(rows):
+        here = jnp.where((row & ((1 << short[0]) - 1)) == 0, 1.0, 0.0)
+        out_ref[row * depth : (row + 1) * depth, :] = here * held * gathered[row * depth : (row + 1) * depth, :]
 
 
 def body(values, levels, coefficients):
@@ -289,6 +280,7 @@
             pltpu.VMEM((local_rows + 1, depth, lanes), jnp.float32),
             pltpu.VMEM((local_rows * depth, lanes), jnp.float32),
             pltpu.VMEM((local_rows * depth, lanes), jnp.float32),
+            pltpu.VMEM((local_rows * depth, lanes), jnp.float32),
             pltpu.SemaphoreType.DMA((local_rows, 2 * steps)),
             pltpu.SemaphoreType.DMA((local_rows, 2 * steps)),
             pltpu.SemaphoreType.DMA,
@@ -298,11 +290,7 @@
             collective_id=0, has_side_effects=True, vmem_limit_bytes=40 * 1024 * 1024
         ),
     )(grid_data.reshape(local_rows, depth, lanes), levels, coefficients, inner, lane)
-    holding = (
-        split_rows_mask(level_row[0], local_rows, grid_data.ndim)
-        * holding_mask(level_row[1:], extents)[None]
-    )
-    return (holding * combined.reshape(grid_data.shape))[None]
+    return combined.reshape(grid_data.shape)[None]
 
 
 def solution(mesh):

time: 54 us -> 48.1 us (0.89)
  between operations: 4.49 us -> 0.67 us
  other arithmetic: 1.98 us -> 0 us
    mul x2 -> x0, other arithmetic: 1.84 us -> none  [the longest x1 1.66 us: body(): return (holding * combined.reshape(grid_data.shape))[None]]
    slice x1 -> x0, local copies, waits for them, and re-layouts: 1.56 us -> none  [body(): level_row[0]]
    unnamed x8 -> x9, local copies, waits for them, and re-layouts: 4.4 us -> 5.72 us
where the time goes in v3:
time: 48.1 us; the launch traced here: 47.6 us
  Pallas kernels  41.2 us (86%)
  local copies, waits for them, and re-layouts  5.72 us (12%)
  between operations  0.67 us (1%)
    pallas_call x1, Pallas kernels, body(): pl.pallas_call(functools.partial(kernel, groups, members, tops), out_shap...  41.2 us
    unnamed x9, local copies, waits for them, and re-layouts  5.72 us

profile of v3, /device:TPU:0, one launch (start us, length us, event | category | flops | bytes accessed | tf_op | source)
XLA Modules:
  0.0 47.6 jit_solution(545271400043331796)
XLA Ops:
  0.7 0.0 copy-start
  0.7 1.6 %copy-done = f32[1,4,4,4,8,8,128]{6,5,4,3,2,1,0:T(8,128)S(1)} copy-done((f32[1,4,4,4,8,8,128]{6,5,4,3,2,1,0:T(8,128)S(1)}, f32[1,4,4,4,8,8,128]{6,5,4,3,2,1,0:T(8,128)}, u32[]{:S(2)}) %copy-start) | copy-done | bytes 2097176
  2.2 0.0 copy-start.1
  2.2 1.3 %copy-done.1 = bf16[9,256,256]{2,1,0:T(8,128)(2,1)S(1)} copy-done((bf16[9,256,256]{2,1,0:T(8,128)(2,1)S(1)}, bf16[9,256,256]{2,1,0:T(8,128)(2,1)}, u32[]{:S(2)}) %copy-start.1) | copy-done | bytes 1179672
  3.5 0.0 copy-start.2
  3.5 0.9 %copy-done.2 = bf16[3,128,128]{2,1,0:T(8,128)(2,1)S(1)} copy-done((bf16[3,128,128]{2,1,0:T(8,128)(2,1)S(1)}, bf16[3,128,128]{2,1,0:T(8,128)(2,1)}, u32[]{:S(2)}) %copy-start.2) | copy-done | bytes 98328
  4.4 0.0 copy-start.3
  4.4 0.7 %copy-done.3 = s32[1,6]{1,0:T(1,128)S(1)} copy-done((s32[1,6]{1,0:T(1,128)S(1)}, s32[1,6]{1,0:T(1,128)}, u32[]{:S(2)}) %copy-start.3) | copy-done | bytes 48
  5.1 41.2 %shard_map.55 = f32[4096,128]{1,0:T(8,128)S(1)} custom-call(f32[4,1024,128]{2,1,0:T(8,128)S(1)} %bitcast.3, s32[1,6]{1,0:T(1,128)S(1)} %copy-done.3, s32[1]{0:T(128)S(6)} %copy.7.weight_ref, bf16[9,256,256]{2,1,0:T(8,128)(2,1)S(1)} %copy-done.1, bf16[3,128,128]{2,1,0:T(8,128)(2,1)S(1)} %copy-done.2), custom_call_target="tpu_custom_call" | custom-call | tf_op jit(solution)/shard_map/pallas_call | solution.py:273
  46.3 1.3 %copy.8 = f32[1,4,4,4,8,8,128]{6,5,4,3,2,1,0:T(8,128)} copy(f32[1,4,4,4,8,8,128]{6,5,4,3,2,1,0:T(8,128)S(1)} %bitcast.2) | data formatting | bytes 4194304
Async XLA Ops:
  0.7 1.6 %copy-start = (f32[1,4,4,4,8,8,128]{6,5,4,3,2,1,0:T(8,128)S(1)}, f32[1,4,4,4,8,8,128]{6,5,4,3,2,1,0:T(8,128)}, u32[]{:S(2)}) copy-start(f32[1,4,4,4,8,8,128]{6,5,4,3,2,1,0:T(8,128)} %param.5) | copy-start | bytes 6291460
  2.2 1.3 %copy-start.1 = (bf16[9,256,256]{2,1,0:T(8,128)(2,1)S(1)}, bf16[9,256,256]{2,1,0:T(8,128)(2,1)}, u32[]{:S(2)}) copy-start(bf16[9,256,256]{2,1,0:T(8,128)(2,1)} %constant.4.clone.inner_ref) | copy-start | bytes 3538948
  3.5 0.9 %copy-start.2 = (bf16[3,128,128]{2,1,0:T(8,128)(2,1)S(1)}, bf16[3,128,128]{2,1,0:T(8,128)(2,1)}, u32[]{:S(2)}) copy-start(bf16[3,128,128]{2,1,0:T(8,128)(2,1)} %constant.5.clone.lane_ref) | copy-start | bytes 294916
  4.4 0.7 %copy-start.3 = (s32[1,6]{1,0:T(1,128)S(1)}, s32[1,6]{1,0:T(1,128)}, u32[]{:S(2)}) copy-start(s32[1,6]{1,0:T(1,128)} %level_ref.1) | copy-start | bytes 76

commit v4 on v3

--- a/solution.py
+++ b/solution.py
@@ -152,14 +152,18 @@
         pl.semaphore_signal(barrier, inc=1, device_id={"dom": near}, device_id_type=MESH)
     pl.semaphore_wait(barrier, steps + 2)
 
-    shift = pltpu.make_async_remote_copy(
-        src_ref=v_ref.at[0], dst_ref=follow, send_sem=z_send, recv_sem=z_recv,
-        device_id={"dom": before}, device_id_type=MESH,
-    )
-    shift.start()
-
     outer = tops[1]
     span = depth // outer
+    shifts = []
+    for i in range(outer):
+        piece = pl.ds(i * span, span)
+        shift = pltpu.make_async_remote_copy(
+            src_ref=v_ref.at[0, piece], dst_ref=follow.at[piece],
+            send_sem=z_send.at[i], recv_sem=z_recv.at[i],
+            device_id={"dom": before}, device_id_type=MESH,
+        )
+        shift.start()
+        shifts.append(shift)
     outer_at = pick(projection_tables(outer), short[1])
     row_at = pick(row_tables(rows), short[0])
     weight = weight_ref[0].astype(jnp.float32)
@@ -172,10 +176,22 @@
         mixed = []
         for i in range(outer):
             total = outer_at[i][0] * blocks[0]
-            for j in range(1, outer):
+            for j in range(1, i + 1):
                 total = total + outer_at[i][j] * blocks[j]
             mixed.append(total)
         return split_dot(jnp.concatenate(mixed, axis=0), right=lane)
+
+    def finish(index):
+        if index == 0:
+            out_ref[0:depth, :] = held * gathered[0:depth, :]
+            return
+        block = index - 1
+        for row in range(1, rows):
+            at = depth + (block * (rows - 1) + row - 1) * span
+            here = jnp.where((row & ((1 << short[0]) - 1)) == 0, 1.0, 0.0)
+            out_ref[row * depth + block * span : row * depth + (block + 1) * span, :] = (
+                here * held[block * span : (block + 1) * span] * gathered[at : at + span, :]
+            )
 
     def reduce_chunk(index, start, size):
         low, now = start, size
@@ -213,6 +229,7 @@
             yield
             copy.wait()
             now *= 2
+        finish(index)
 
     place = lax.broadcasted_iota(jnp.int32, (depth, lanes), 0)
     inside = lax.broadcasted_iota(jnp.int32, (depth, lanes), 1) < (lanes >> short[5])
@@ -229,23 +246,29 @@
     next(head)
     for row in range(1, rows):
         part[row] = project(v_ref[row])
-    next(head)
-    shift.wait()
-    part[rows] = project(follow[...])
     active = [head]
-    for row in range(1, rows):
-        total = row_at[row][0] * part[0]
-        for source in range(1, rows + 1):
-            total = total + row_at[row][source] * part[source]
-        acc[row * depth : (row + 1) * depth, :] = total
-        chunk = reduce_chunk(row, row * depth, depth)
+    taken = []
+    for block in range(outer):
+        shifts[block].wait()
+        here = slice(block * span, (block + 1) * span)
+        taken.append(split_dot(follow[here, :], left=inner))
+        total = outer_at[block][0] * taken[0]
+        for j in range(1, block + 1):
+            total = total + outer_at[block][j] * taken[j]
+        ahead = split_dot(total, right=lane)
+        for row in range(1, rows):
+            total = row_at[row][rows] * ahead
+            for source in range(rows):
+                total = total + row_at[row][source] * part[source, here, :]
+            at = depth + (block * (rows - 1) + row - 1) * span
+            acc[at : at + span, :] = total
+        width = (rows - 1) * span
+        chunk = reduce_chunk(block + 1, depth + block * width, width)
         next(chunk)
+        active = [each for each in active if next(each, "end") != "end"]
         active.append(chunk)
     while active:
         active = [chunk for chunk in active if next(chunk, "end") != "end"]
-    for row in range(rows):
-        here = jnp.where((row & ((1 << short[0]) - 1)) == 0, 1.0, 0.0)
-        out_ref[row * depth : (row + 1) * depth, :] = here * held * gathered[row * depth : (row + 1) * depth, :]
 
 
 def body(values, levels, coefficients):
@@ -277,14 +300,14 @@
         out_specs=vmem,
         scratch_shapes=[
             pltpu.VMEM((depth, lanes), jnp.float32),
-            pltpu.VMEM((local_rows + 1, depth, lanes), jnp.float32),
+            pltpu.VMEM((local_rows, depth, lanes), jnp.float32),
             pltpu.VMEM((local_rows * depth, lanes), jnp.float32),
             pltpu.VMEM((local_rows * depth, lanes), jnp.float32),
             pltpu.VMEM((local_rows * depth, lanes), jnp.float32),
-            pltpu.SemaphoreType.DMA((local_rows, 2 * steps)),
-            pltpu.SemaphoreType.DMA((local_rows, 2 * steps)),
-            pltpu.SemaphoreType.DMA,
-            pltpu.SemaphoreType.DMA,
+            pltpu.SemaphoreType.DMA((extents[0] + 1, 2 * steps)),
+            pltpu.SemaphoreType.DMA((extents[0] + 1, 2 * steps)),
+            pltpu.SemaphoreType.DMA((extents[0],)),
+            pltpu.SemaphoreType.DMA((extents[0],)),
         ],
         compiler_params=pltpu.CompilerParams(
             collective_id=0, has_side_effects=True, vmem_limit_bytes=40 * 1024 * 1024

time: 48.1 us -> 52 us (1.081)
  Pallas kernels: 41.2 us -> 45.4 us
    pallas_call x1, Pallas kernels: 41.2 us -> 45.4 us  [body(): pl.pallas_call(functools.partial(kernel, groups, members, tops), out_shap...]
where the time goes in v4:
time: 52 us; the launch traced here: 51.8 us
  Pallas kernels  45.4 us (87%)
  local copies, waits for them, and re-layouts  5.72 us (11%)
  between operations  0.67 us (1%)
    pallas_call x1, Pallas kernels, body(): pl.pallas_call(functools.partial(kernel, groups, members, tops), out_shap...  45.4 us
    unnamed x9, local copies, waits for them, and re-layouts  5.72 us

profile of v4, /device:TPU:0, one launch (start us, length us, event | category | flops | bytes accessed | tf_op | source)
XLA Modules:
  0.0 51.8 jit_solution(17274126482289247152)
XLA Ops:
  0.7 0.0 copy-start
  0.7 1.6 %copy-done = f32[1,4,4,4,8,8,128]{6,5,4,3,2,1,0:T(8,128)S(1)} copy-done((f32[1,4,4,4,8,8,128]{6,5,4,3,2,1,0:T(8,128)S(1)}, f32[1,4,4,4,8,8,128]{6,5,4,3,2,1,0:T(8,128)}, u32[]{:S(2)}) %copy-start) | copy-done | bytes 2097176
  2.2 0.0 copy-start.1
  2.2 1.3 %copy-done.1 = bf16[9,256,256]{2,1,0:T(8,128)(2,1)S(1)} copy-done((bf16[9,256,256]{2,1,0:T(8,128)(2,1)S(1)}, bf16[9,256,256]{2,1,0:T(8,128)(2,1)}, u32[]{:S(2)}) %copy-start.1) | copy-done | bytes 1179672
  3.5 0.0 copy-start.2
  3.5 0.9 %copy-done.2 = bf16[3,128,128]{2,1,0:T(8,128)(2,1)S(1)} copy-done((bf16[3,128,128]{2,1,0:T(8,128)(2,1)S(1)}, bf16[3,128,128]{2,1,0:T(8,128)(2,1)}, u32[]{:S(2)}) %copy-start.2) | copy-done | bytes 98328
  4.4 0.0 copy-start.3
  4.4 0.7 %copy-done.3 = s32[1,6]{1,0:T(1,128)S(1)} copy-done((s32[1,6]{1,0:T(1,128)S(1)}, s32[1,6]{1,0:T(1,128)}, u32[]{:S(2)}) %copy-start.3) | copy-done | bytes 48
  5.1 45.4 %shard_map.55 = f32[4096,128]{1,0:T(8,128)S(1)} custom-call(f32[4,1024,128]{2,1,0:T(8,128)S(1)} %bitcast.3, s32[1,6]{1,0:T(1,128)S(1)} %copy-done.3, s32[1]{0:T(128)S(6)} %copy.7.weight_ref, bf16[9,256,256]{2,1,0:T(8,128)(2,1)S(1)} %copy-done.1, bf16[3,128,128]{2,1,0:T(8,128)(2,1)S(1)} %copy-done.2), custom_call_target="tpu_custom_call" | custom-call | tf_op jit(solution)/shard_map/pallas_call | solution.py:296
  50.5 1.3 %copy.8 = f32[1,4,4,4,8,8,128]{6,5,4,3,2,1,0:T(8,128)} copy(f32[1,4,4,4,8,8,128]{6,5,4,3,2,1,0:T(8,128)S(1)} %bitcast.2) | data formatting | bytes 4194304
Async XLA Ops:
  0.7 1.6 %copy-start = (f32[1,4,4,4,8,8,128]{6,5,4,3,2,1,0:T(8,128)S(1)}, f32[1,4,4,4,8,8,128]{6,5,4,3,2,1,0:T(8,128)}, u32[]{:S(2)}) copy-start(f32[1,4,4,4,8,8,128]{6,5,4,3,2,1,0:T(8,128)} %param.5) | copy-start | bytes 6291460
  2.2 1.3 %copy-start.1 = (bf16[9,256,256]{2,1,0:T(8,128)(2,1)S(1)}, bf16[9,256,256]{2,1,0:T(8,128)(2,1)}, u32[]{:S(2)}) copy-start(bf16[9,256,256]{2,1,0:T(8,128)(2,1)} %constant.4.clone.inner_ref) | copy-start | bytes 3538948
  3.5 0.9 %copy-start.2 = (bf16[3,128,128]{2,1,0:T(8,128)(2,1)S(1)}, bf16[3,128,128]{2,1,0:T(8,128)(2,1)}, u32[]{:S(2)}) copy-start(bf16[3,128,128]{2,1,0:T(8,128)(2,1)} %constant.5.clone.lane_ref) | copy-start | bytes 294916
  4.4 0.7 %copy-start.3 = (s32[1,6]{1,0:T(1,128)S(1)}, s32[1,6]{1,0:T(1,128)}, u32[]{:S(2)}) copy-start(s32[1,6]{1,0:T(1,128)} %level_ref.1) | copy-start | bytes 76

commit v5 on v3

--- a/solution.py
+++ b/solution.py
@@ -120,9 +120,17 @@
     ]
 
 
-def kernel(groups, members, tops, v_ref, level_ref, weight_ref, inner_ref, lane_ref, out_ref,
-           follow, part, acc, recv, gathered, send_sem, recv_sem, z_send, z_recv):
+def kernel(groups, members, tops, v_hbm, level_ref, weight_ref, inner_hbm, lane_hbm, out_ref,
+           v_ref, inner_ref, lane_ref, load_sem, follow, part, acc, recv, gathered, send_sem, recv_sem, z_send, z_recv):
     rows, depth, lanes = v_ref.shape
+    loads = [
+        pltpu.make_async_copy(v_hbm.at[0], v_ref.at[0], load_sem.at[0]),
+        pltpu.make_async_copy(inner_hbm, inner_ref, load_sem.at[rows]),
+        pltpu.make_async_copy(lane_hbm, lane_ref, load_sem.at[rows + 1]),
+    ]
+    later = [pltpu.make_async_copy(v_hbm.at[row], v_ref.at[row], load_sem.at[row]) for row in range(1, rows)]
+    for load in loads + later:
+        load.start()
     steps = groups.bit_length() - 1
     me = lax.axis_index("grid")
     dom = lax.axis_index("dom")
@@ -153,7 +161,7 @@
     pl.semaphore_wait(barrier, steps + 2)
 
     shift = pltpu.make_async_remote_copy(
-        src_ref=v_ref.at[0], dst_ref=follow, send_sem=z_send, recv_sem=z_recv,
+        src_ref=v_hbm.at[0], dst_ref=follow, send_sem=z_send, recv_sem=z_recv,
         device_id={"dom": before}, device_id_type=MESH,
     )
     shift.start()
@@ -164,6 +172,8 @@
     row_at = pick(row_tables(rows), short[0])
     weight = weight_ref[0].astype(jnp.float32)
     row_at = [[weight * entry for entry in line] for line in row_at]
+    for load in loads:
+        load.wait()
     inner = inner_ref[short[2]] * inner_ref[SHORTFALLS + short[3]] * inner_ref[2 * SHORTFALLS + short[4]]
     lane = lane_ref[short[5]]
 
@@ -228,7 +238,9 @@
     head = reduce_chunk(0, 0, depth)
     next(head)
     for row in range(1, rows):
+        later[row - 1].wait()
         part[row] = project(v_ref[row])
+        next(head)
     next(head)
     shift.wait()
     part[rows] = project(follow[...])
@@ -269,13 +281,18 @@
 
     steps = groups.bit_length() - 1
     vmem = pl.BlockSpec(memory_space=pltpu.VMEM)
+    hbm = pl.BlockSpec(memory_space=pltpu.HBM)
     smem = pl.BlockSpec(memory_space=pltpu.SMEM)
     combined = pl.pallas_call(
         functools.partial(kernel, groups, members, tops),
         out_shape=jax.ShapeDtypeStruct((local_rows * depth, lanes), jnp.float32),
-        in_specs=[vmem, smem, smem, vmem, vmem],
+        in_specs=[hbm, smem, smem, hbm, hbm],
         out_specs=vmem,
         scratch_shapes=[
+            pltpu.VMEM((local_rows, depth, lanes), jnp.float32),
+            pltpu.VMEM(inner.shape, jnp.bfloat16),
+            pltpu.VMEM(lane.shape, jnp.bfloat16),
+            pltpu.SemaphoreType.DMA((local_rows + 2,)),
             pltpu.VMEM((depth, lanes), jnp.float32),
             pltpu.VMEM((local_rows + 1, depth, lanes), jnp.float32),
             pltpu.VMEM((local_rows * depth, lanes), jnp.float32),
@@ -287,7 +304,7 @@
             pltpu.SemaphoreType.DMA,
         ],
         compiler_params=pltpu.CompilerParams(
-            collective_id=0, has_side_effects=True, vmem_limit_bytes=40 * 1024 * 1024
+            collective_id=0, has_side_effects=True, vmem_limit_bytes=61 * 1024 * 1024
         ),
     )(grid_data.reshape(local_rows, depth, lanes), levels, coefficients, inner, lane)
     return combined.reshape(grid_data.shape)[None]

time: 48.1 us -> 52.1 us (1.083)
  Pallas kernels: 41.2 us -> 48.1 us
  local copies, waits for them, and re-layouts: 5.72 us -> 3.16 us
    pallas_call x1, Pallas kernels: 41.2 us -> 48.1 us  [body(): pl.pallas_call(functools.partial(kernel, groups, members, tops), out_shap...]
    unnamed x9 -> x1, local copies, waits for them, and re-layouts: 5.72 us -> 3.16 us
where the time goes in v5:
time: 52.1 us; the launch traced here: 51.9 us
  Pallas kernels  48.1 us (92%)
  local copies, waits for them, and re-layouts  3.16 us (6%)
  between operations  0.66 us (1%)
    pallas_call x1, Pallas kernels, body(): pl.pallas_call(functools.partial(kernel, groups, members, tops), out_shap...  48.1 us
    unnamed x1, local copies, waits for them, and re-layouts  3.16 us

profile of v5, /device:TPU:0, one launch (start us, length us, event | category | flops | bytes accessed | tf_op | source)
XLA Modules:
  0.0 51.9 jit_solution(17950715743156730118)
XLA Ops:
  0.7 48.1 %shard_map.55 = f32[4096,128]{1,0:T(8,128)} custom-call(f32[4,1024,128]{2,1,0:T(8,128)} %bitcast.3, s32[1,6]{1,0:T(1,128)} %level_ref.1, s32[1]{0:T(128)S(6)} %copy.7.weight_ref, bf16[9,256,256]{2,1,0:T(8,128)(2,1)} %constant.4.clone.inner_hbm, bf16[3,128,128]{2,1,0:T(8,128)(2,1)} %constant.5.clone.lane_hbm), custom_call_target="tpu_custom_call" | custom-call | tf_op jit(solution)/shard_map/pallas_call | solution.py:286
  48.7 3.2 %copy.8 = f32[1,4,4,4,8,8,128]{6,5,4,3,2,1,0:T(8,128)} copy(f32[1,4,4,4,8,8,128]{6,5,4,3,2,1,0:T(8,128)} %bitcast.2) | data formatting | bytes 4194304

commit v6 on v3

--- a/solution.py
+++ b/solution.py
@@ -102,13 +102,11 @@
 def split_dot(data, right=None, left=None):
     high = data.astype(jnp.bfloat16)
     low = (data - high.astype(jnp.float32)).astype(jnp.bfloat16)
+    both = jnp.concatenate([high, low], axis=1)
     if right is not None:
-        return jnp.dot(high, right, preferred_element_type=jnp.float32) + jnp.dot(
-            low, right, preferred_element_type=jnp.float32
-        )
-    return jnp.dot(left, high, preferred_element_type=jnp.float32) + jnp.dot(
-        left, low, preferred_element_type=jnp.float32
-    )
+        return jnp.dot(both, jnp.concatenate([right, right], axis=0), preferred_element_type=jnp.float32)
+    result = jnp.dot(left, both, preferred_element_type=jnp.float32)
+    return result[:, : data.shape[1]] + result[:, data.shape[1] :]
 
 
 def pick(tables, short):

time: 48.1 us -> 47.8 us (level)
  no operation moved by 1% of the time
where the time goes in v6:
time: 47.8 us; the launch traced here: 47.4 us
  Pallas kernels  41 us (86%)
  local copies, waits for them, and re-layouts  5.72 us (12%)
  between operations  0.67 us (1%)
    pallas_call x1, Pallas kernels, body(): pl.pallas_call(functools.partial(kernel, groups, members, tops), out_shap...  41 us
    unnamed x9, local copies, waits for them, and re-layouts  5.72 us

profile of v6, /device:TPU:0, one launch (start us, length us, event | category | flops | bytes accessed | tf_op | source)
XLA Modules:
  0.0 47.4 jit_solution(8925341412899875721)
XLA Ops:
  0.7 0.0 copy-start
  0.7 1.6 %copy-done = f32[1,4,4,4,8,8,128]{6,5,4,3,2,1,0:T(8,128)S(1)} copy-done((f32[1,4,4,4,8,8,128]{6,5,4,3,2,1,0:T(8,128)S(1)}, f32[1,4,4,4,8,8,128]{6,5,4,3,2,1,0:T(8,128)}, u32[]{:S(2)}) %copy-start) | copy-done | bytes 2097176
  2.2 0.0 copy-start.1
  2.2 1.3 %copy-done.1 = bf16[9,256,256]{2,1,0:T(8,128)(2,1)S(1)} copy-done((bf16[9,256,256]{2,1,0:T(8,128)(2,1)S(1)}, bf16[9,256,256]{2,1,0:T(8,128)(2,1)}, u32[]{:S(2)}) %copy-start.1) | copy-done | bytes 1179672
  3.5 0.0 copy-start.2
  3.5 0.9 %copy-done.2 = bf16[3,128,128]{2,1,0:T(8,128)(2,1)S(1)} copy-done((bf16[3,128,128]{2,1,0:T(8,128)(2,1)S(1)}, bf16[3,128,128]{2,1,0:T(8,128)(2,1)}, u32[]{:S(2)}) %copy-start.2) | copy-done | bytes 98328
  4.4 0.0 copy-start.3
  4.4 0.7 %copy-done.3 = s32[1,6]{1,0:T(1,128)S(1)} copy-done((s32[1,6]{1,0:T(1,128)S(1)}, s32[1,6]{1,0:T(1,128)}, u32[]{:S(2)}) %copy-start.3) | copy-done | bytes 48
  5.1 41.0 %shard_map.55 = f32[4096,128]{1,0:T(8,128)S(1)} custom-call(f32[4,1024,128]{2,1,0:T(8,128)S(1)} %bitcast.3, s32[1,6]{1,0:T(1,128)S(1)} %copy-done.3, s32[1]{0:T(128)S(6)} %copy.7.weight_ref, bf16[9,256,256]{2,1,0:T(8,128)(2,1)S(1)} %copy-done.1, bf16[3,128,128]{2,1,0:T(8,128)(2,1)S(1)} %copy-done.2), custom_call_target="tpu_custom_call" | custom-call | tf_op jit(solution)/shard_map/pallas_call | solution.py:271
  46.1 1.3 %copy.8 = f32[1,4,4,4,8,8,128]{6,5,4,3,2,1,0:T(8,128)} copy(f32[1,4,4,4,8,8,128]{6,5,4,3,2,1,0:T(8,128)S(1)} %bitcast.2) | data formatting | bytes 4194304
Async XLA Ops:
  0.7 1.6 %copy-start = (f32[1,4,4,4,8,8,128]{6,5,4,3,2,1,0:T(8,128)S(1)}, f32[1,4,4,4,8,8,128]{6,5,4,3,2,1,0:T(8,128)}, u32[]{:S(2)}) copy-start(f32[1,4,4,4,8,8,128]{6,5,4,3,2,1,0:T(8,128)} %param.5) | copy-start | bytes 6291460
  2.2 1.3 %copy-start.1 = (bf16[9,256,256]{2,1,0:T(8,128)(2,1)S(1)}, bf16[9,256,256]{2,1,0:T(8,128)(2,1)}, u32[]{:S(2)}) copy-start(bf16[9,256,256]{2,1,0:T(8,128)(2,1)} %constant.4.clone.inner_ref) | copy-start | bytes 3538948
  3.5 0.9 %copy-start.2 = (bf16[3,128,128]{2,1,0:T(8,128)(2,1)S(1)}, bf16[3,128,128]{2,1,0:T(8,128)(2,1)}, u32[]{:S(2)}) copy-start(bf16[3,128,128]{2,1,0:T(8,128)(2,1)} %constant.5.clone.lane_ref) | copy-start | bytes 294916
  4.4 0.7 %copy-start.3 = (s32[1,6]{1,0:T(1,128)S(1)}, s32[1,6]{1,0:T(1,128)}, u32[]{:S(2)}) copy-start(s32[1,6]{1,0:T(1,128)} %level_ref.1) | copy-start | bytes 76

commit v7 on v6

--- a/solution.py
+++ b/solution.py
@@ -229,6 +229,7 @@
         part[row] = project(v_ref[row])
     next(head)
     shift.wait()
+    next(head)
     part[rows] = project(follow[...])
     active = [head]
     for row in range(1, rows):

time: 47.8 us -> 49.8 us (1.042)
  Pallas kernels: 41 us -> 43.2 us
    pallas_call x1, Pallas kernels: 41 us -> 43.2 us  [body(): pl.pallas_call(functools.partial(kernel, groups, members, tops), out_shap...]
where the time goes in v7:
time: 49.8 us; the launch traced here: 49.6 us
  Pallas kernels  43.2 us (87%)
  local copies, waits for them, and re-layouts  5.72 us (11%)
  between operations  0.67 us (1%)
    pallas_call x1, Pallas kernels, body(): pl.pallas_call(functools.partial(kernel, groups, members, tops), out_shap...  43.2 us
    unnamed x9, local copies, waits for them, and re-layouts  5.72 us

profile of v7, /device:TPU:0, one launch (start us, length us, event | category | flops | bytes accessed | tf_op | source)
XLA Modules:
  0.0 49.6 jit_solution(14796823791898091354)
XLA Ops:
  0.7 0.0 copy-start
  0.7 1.6 %copy-done = f32[1,4,4,4,8,8,128]{6,5,4,3,2,1,0:T(8,128)S(1)} copy-done((f32[1,4,4,4,8,8,128]{6,5,4,3,2,1,0:T(8,128)S(1)}, f32[1,4,4,4,8,8,128]{6,5,4,3,2,1,0:T(8,128)}, u32[]{:S(2)}) %copy-start) | copy-done | bytes 2097176
  2.2 0.0 copy-start.1
  2.2 1.3 %copy-done.1 = bf16[9,256,256]{2,1,0:T(8,128)(2,1)S(1)} copy-done((bf16[9,256,256]{2,1,0:T(8,128)(2,1)S(1)}, bf16[9,256,256]{2,1,0:T(8,128)(2,1)}, u32[]{:S(2)}) %copy-start.1) | copy-done | bytes 1179672
  3.5 0.0 copy-start.2
  3.5 0.9 %copy-done.2 = bf16[3,128,128]{2,1,0:T(8,128)(2,1)S(1)} copy-done((bf16[3,128,128]{2,1,0:T(8,128)(2,1)S(1)}, bf16[3,128,128]{2,1,0:T(8,128)(2,1)}, u32[]{:S(2)}) %copy-start.2) | copy-done | bytes 98328
  4.4 0.0 copy-start.3
  4.4 0.7 %copy-done.3 = s32[1,6]{1,0:T(1,128)S(1)} copy-done((s32[1,6]{1,0:T(1,128)S(1)}, s32[1,6]{1,0:T(1,128)}, u32[]{:S(2)}) %copy-start.3) | copy-done | bytes 48
  5.1 43.2 %shard_map.55 = f32[4096,128]{1,0:T(8,128)S(1)} custom-call(f32[4,1024,128]{2,1,0:T(8,128)S(1)} %bitcast.3, s32[1,6]{1,0:T(1,128)S(1)} %copy-done.3, s32[1]{0:T(128)S(6)} %copy.7.weight_ref, bf16[9,256,256]{2,1,0:T(8,128)(2,1)S(1)} %copy-done.1, bf16[3,128,128]{2,1,0:T(8,128)(2,1)S(1)} %copy-done.2), custom_call_target="tpu_custom_call" | custom-call | tf_op jit(solution)/shard_map/pallas_call | solution.py:272
  48.2 1.3 %copy.8 = f32[1,4,4,4,8,8,128]{6,5,4,3,2,1,0:T(8,128)} copy(f32[1,4,4,4,8,8,128]{6,5,4,3,2,1,0:T(8,128)S(1)} %bitcast.2) | data formatting | bytes 4194304
Async XLA Ops:
  0.7 1.6 %copy-start = (f32[1,4,4,4,8,8,128]{6,5,4,3,2,1,0:T(8,128)S(1)}, f32[1,4,4,4,8,8,128]{6,5,4,3,2,1,0:T(8,128)}, u32[]{:S(2)}) copy-start(f32[1,4,4,4,8,8,128]{6,5,4,3,2,1,0:T(8,128)} %param.5) | copy-start | bytes 6291460
  2.2 1.3 %copy-start.1 = (bf16[9,256,256]{2,1,0:T(8,128)(2,1)S(1)}, bf16[9,256,256]{2,1,0:T(8,128)(2,1)}, u32[]{:S(2)}) copy-start(bf16[9,256,256]{2,1,0:T(8,128)(2,1)} %constant.4.clone.inner_ref) | copy-start | bytes 3538948
  3.5 0.9 %copy-start.2 = (bf16[3,128,128]{2,1,0:T(8,128)(2,1)S(1)}, bf16[3,128,128]{2,1,0:T(8,128)(2,1)}, u32[]{:S(2)}) copy-start(bf16[3,128,128]{2,1,0:T(8,128)(2,1)} %constant.5.clone.lane_ref) | copy-start | bytes 294916
  4.4 0.7 %copy-start.3 = (s32[1,6]{1,0:T(1,128)S(1)}, s32[1,6]{1,0:T(1,128)}, u32[]{:S(2)}) copy-start(s32[1,6]{1,0:T(1,128)} %level_ref.1) | copy-start | bytes 76
